TPU v7x, 128 devices: a whole 4x4x4 slice. The times are simulated.
128 devices in a mesh: dp: 32 (over x, y, z_hi), fsdp: 4 (over z_lo, core).
Axes of the slice: x: 4, y: 4, z: 4 (z_hi: 2, z_lo: 2; z = z_hi * 2 + z_lo), core: 2. Of those that a mesh axis runs over, the one named last changes fastest.
Arguments:
- image_feat: bfloat16 [98304, 1152], P(('dp', 'fsdp')), may hold values from -6 to 6
- text_emb: bfloat16 [98304, 1152], P(('dp', 'fsdp')), may hold values from -0.1875 to 0.1875
- head: bfloat16 [1152, 1152], P('fsdp'), may hold values from -0.0048828125 to 0.0048828125
- partner: int32 [98304], P(('dp', 'fsdp')), may hold values from 0 to 767, as said below
- scale: float32 [1], replicated, may hold values from 5 to 15
- bias: float32 [1], replicated, may hold values from -4 to -1
Outputs:
- head_grad: float32 [1152, 1152], P('fsdp')
- text_grad: float32 [98304, 1152], P(('dp', 'fsdp'))
Inputs may be any that keep to these rules, and one draw needn't show every extreme that they name: `partner`: within each block of 768 rows every value appears exactly once.
All inputs are finite; a program needn't handle non-finite values.
Results may differ from a plain program's by a relative error of at most 0.0051.
Values may be sent and summed in bfloat16 or wider, within the bound.
No kernel may reach another device: no remote copies, remote signals or barrier semaphores. Data moves between devices by JAX's collectives and lax.ppermute only.
A program may use at most 128 MiB of HBM per device.

v0:
```python
import jax
import jax.numpy as jnp
from jax import lax
from jax.sharding import PartitionSpec as P

STEPS = 4


def passed_along(value, axis, by):
    length = lax.axis_size(axis)
    return lax.ppermute(value, axis, [(i, (i + by) % length) for i in range(length)])


def unit_rows(vec):
    inv = lax.rsqrt(jnp.sum(vec * vec, axis=-1, keepdims=True) + 1e-06)
    return (vec * inv, inv)


def on_device(image_feat, text_emb, head, partner, scale, bias):
    rows = image_feat.shape[0]
    width = head.shape[1]
    columns = image_feat
    proj = jnp.dot(
        columns,
        lax.all_gather(head, "fsdp", axis=0, tiled=True),
        preferred_element_type=jnp.float32,
    )
    img_unit, rx = unit_rows(proj)
    img_b = img_unit.astype(jnp.bfloat16)
    txt_unit, ry = unit_rows(text_emb.astype(jnp.float32))
    txt_b = txt_unit.astype(jnp.bfloat16)
    temper = scale[0]
    offset = bias[0]
    onehot = (partner[:, None] == jnp.arange(rows, dtype=jnp.int32)[None, :]).astype(jnp.float32)
    contract_rows = (((0,), (0,)), ((), ()))
    visiting = txt_b
    d_img = jnp.zeros((rows, width), jnp.float32)
    text_total = jnp.zeros((rows, width), jnp.float32)
    for step in range(STEPS):
        if step > 0:
            visiting = passed_along(visiting, "dp", 1)
        logits = temper * jnp.dot(img_b, visiting.T, preferred_element_type=jnp.float32) + offset
        if step == 0:
            target = onehot
        else:
            target = jnp.zeros_like(onehot)
        grad_b = (jax.nn.sigmoid(logits) - target).astype(jnp.bfloat16)
        d_img = d_img + jnp.dot(grad_b, visiting, preferred_element_type=jnp.float32)
        text_part = lax.dot_general(
            grad_b, img_b, contract_rows, preferred_element_type=jnp.float32
        )
        if step > 0:
            text_total = passed_along(text_total, "dp", 1) + text_part
        else:
            text_total = text_part
    text_total = passed_along(text_total, "dp", -(STEPS - 1))
    d_img = temper * d_img
    d_proj = rx * (d_img - img_unit * jnp.sum(img_unit * d_img, axis=-1, keepdims=True))
    d_proj = d_proj.astype(jnp.bfloat16)
    columns = image_feat
    head_part = lax.psum_scatter(
        lax.dot_general(columns, d_proj, contract_rows, preferred_element_type=jnp.float32),
        "fsdp",
        scatter_dimension=0,
        tiled=True,
    )
    head_grad = lax.psum(head_part, "dp") / rows
    d_txt = temper * text_total
    text_grad = ry * (d_txt - txt_unit * jnp.sum(txt_unit * d_txt, axis=-1, keepdims=True))
    return (head_grad, text_grad)


def solution(mesh):
    in_specs = (
        P(("dp", "fsdp"), None),
        P(("dp", "fsdp"), None),
        P("fsdp", None),
        P(("dp", "fsdp")),
        P(),
        P(),
    )
    out_specs = (P("fsdp", None), P(("dp", "fsdp"), None))
    return jax.shard_map(
        on_device, mesh=mesh, in_specs=in_specs, out_specs=out_specs, check_vma=False
    )
```

profile of v0, /device:TPU:0, one launch (start us, length us, event | category | flops | bytes accessed | tf_op | source)
XLA Modules:
  0.0 879.0 jit_solution(4176961852424788695)
XLA Ops:
  7.2 0.0 copy-start
  7.2 0.0 copy-start.1
  7.2 0.0 all-gather.2.cloned.1.call-start
  7.2 0.7 all-gather.2.cloned.1.call-update
  7.9 0.0 reduce-scatter.4.cloned.1.call-start
  8.0 1.9 fusion.7
  9.9 0.0 copy-done.1
  9.9 0.4 fusion.2
  10.2 0.0 copy-start.4
  10.3 1.2 copy-done.4
  11.5 4.0 collective-permute-start
  15.4 59.2 %collective-permute-done = bf16[768,1152]{1,0:T(8,128)(2,1)S(1)} collective-permute-done((bf16[768,1152]{1,0:T(8,128)(2,1)S(1)}, bf16[768,1152]{1,0:T(8,128)(2,1)S(1)}, u32[]{:S(2)}, u32[]{:S(2)}) %collective-permute-start) | collective-permute-done | bytes 1769504 | tf_op jit(solution)/shard_map/ppermute | solution.py:11
  74.6 1.2 copy-done.8
  75.8 4.0 collective-permute-start.1
  81.1 41.2 %collective-permute-done.1 = bf16[768,1152]{1,0:T(8,128)(2,1)} collective-permute-done((bf16[768,1152]{1,0:T(8,128)(2,1)S(1)}, bf16[768,1152]{1,0:T(8,128)(2,1)}, u32[]{:S(2)}, u32[]{:S(2)}) %collective-permute-start.1) | collective-permute-done | bytes 1769504 | tf_op jit(solution)/shard_map/ppermute | solution.py:11
  122.3 0.0 collective-permute-start.2
  122.3 0.0 copy-done
  122.3 4.5 multiply_reduce_fusion.1
  126.8 0.0 copy-start.5
  126.8 0.0 copy-start.10
  126.8 0.3 multiply_convert_fusion.1
  127.1 0.0 copy-start.2
  127.1 1.7 copy-done.5
  128.9 0.0 copy-done.10
  128.9 2.0 subtract_convert_fusion
  130.9 1.7 fusion.10
  132.6 0.0 copy-start.9
  132.6 3.5 fusion.11
  136.1 0.1 collective-permute-start.3
  136.1 1.9 divide_convert_fusion.2
  138.1 0.0 copy-start.13
  138.1 1.8 convolution_add_fusion.3
  139.9 3.4 divide_convert_fusion.1
  143.3 3.7 convolution_add_fusion.2
  147.1 22.8 %collective-permute-done.2 = bf16[768,1152]{1,0:T(8,128)(2,1)} collective-permute-done((bf16[768,1152]{1,0:T(8,128)(2,1)}, bf16[768,1152]{1,0:T(8,128)(2,1)}, u32[]{:S(2)}, u32[]{:S(2)}) %collective-permute-start.2) | collective-permute-done | bytes 1769504 | tf_op jit(solution)/shard_map/ppermute | solution.py:11
  169.9 3.4 divide_convert_fusion
  173.3 3.8 multiply_reduce_fusion
  177.1 5.1 convolution_bitcast_fusion
  182.3 6.9 copy.10
  189.1 0.0 reduce-scatter.4.cloned.1.call-update
  189.1 0.3 all-reduce.2.cloned.1.call-start
  189.4 0.0 copy-start.3
  189.4 0.0 copy-start.12
  189.4 88.3 %collective-permute-done.3 = f32[768,1152]{1,0:T(8,128)} collective-permute-done((f32[768,1152]{1,0:T(8,128)}, f32[768,1152]{1,0:T(8,128)}, u32[]{:S(2)}, u32[]{:S(2)}) %collective-permute-start.3) | collective-permute-done | bytes 3538976 | tf_op jit(solution)/shard_map/ppermute | solution.py:11
  277.7 4.9 convolution_add_fusion
  282.6 3.9 collective-permute-start.4
  286.6 0.0 copy-done.12
  286.6 1.7 fusion.12
  288.3 74.0 %collective-permute-done.4 = f32[768,1152]{1,0:T(8,128)S(1)} collective-permute-done((f32[768,1152]{1,0:T(8,128)S(1)}, f32[768,1152]{1,0:T(8,128)S(1)}, u32[]{:S(2)}, u32[]{:S(2)}) %collective-permute-start.4) | collective-permute-done | bytes 3538976 | tf_op jit(solution)/shard_map/ppermute | solution.py:11
  362.4 0.4 add.83
  362.7 0.2 collective-permute-start.5
  362.9 0.0 copy-done.7
  362.9 1.7 fusion.13
  364.6 76.9 %collective-permute-done.5 = f32[768,1152]{1,0:T(8,128)S(1)} collective-permute-done((f32[768,1152]{1,0:T(8,128)S(1)}, f32[768,1152]{1,0:T(8,128)S(1)}, u32[]{:S(2)}, u32[]{:S(2)}) %collective-permute-start.5) | collective-permute-done | bytes 3538976 | tf_op jit(solution)/shard_map/ppermute | solution.py:11
  441.5 2.1 add.84
  443.7 0.0 collective-permute-start.6
  443.7 3.1 copy.11
  446.8 0.0 all-reduce.2.cloned.1.call-update
  446.8 412.5 %all-reduce.2.cloned.1.call-done = f32[288,1152]{0,1:T(8,128)} async-done(((f32[288,1152]{0,1:T(8,128)}), f32[288,1152]{0,1:T(8,128)}) %all-reduce.2.cloned.1.call-update) | async-done | bytes 1327120 | tf_op jit(solution)/shard_map/psum | solution.py:67
  859.3 2.8 broadcast_multiply_fusion
  862.2 3.0 copy.9
  865.2 0.0 collective-permute-done.6
  865.2 2.7 fusion.4
  867.9 4.5 fusion.6
  (14 shorter events, 0.0 us)
Async XLA Ops:
  7.2 115.1 %copy-start = (bf16[768,1152]{1,0:T(8,128)(2,1)S(1)}, bf16[768,1152]{1,0:T(8,128)(2,1)}, u32[]{:S(2)}) copy-start(bf16[768,1152]{1,0:T(8,128)(2,1)} %param.6) | copy-start | bytes 5308420
  7.2 2.7 copy-start.1
  7.2 115.1 %all-gather.2.cloned.1.call-start = ((), (), s32[]{:S(2)}) async-start(), calls=%async_computation.1 | async-start | bytes 3317760 | tf_op jit(solution)/shard_map/all_gather | solution.py:25
  7.9 435.8 %reduce-scatter.4.cloned.1.call-start = ((), (), s32[]{:S(2)}) async-start(), calls=%async_computation.3 | async-start | bytes 6635520
  10.2 1.2 copy-start.4
  11.5 63.2 %collective-permute-start = (bf16[768,1152]{1,0:T(8,128)(2,1)S(1)}, bf16[768,1152]{1,0:T(8,128)(2,1)S(1)}, u32[]{:S(2)}, u32[]{:S(2)}) collective-permute-start(bf16[768,1152]{1,0:T(8,128)(2,1)S(1)} %fusion.2), channel_id=1, source_target_pairs={{0,4},{4,8},{8,12},{12,16},{16,20},{20,24},{24,28},{28,32},{32,36}... | collective-permute-start | bytes 5308424 | tf_op jit(solution)/shard_map/ppermute | solution.py:11
  74.6 1.2 copy-start.8
  75.8 46.5 %collective-permute-start.1 = (bf16[768,1152]{1,0:T(8,128)(2,1)S(1)}, bf16[768,1152]{1,0:T(8,128)(2,1)}, u32[]{:S(2)}, u32[]{:S(2)}) collective-permute-start(bf16[768,1152]{1,0:T(8,128)(2,1)S(1)} %collective-permute-done), channel_id=1, source_target_pairs={{0,4},{4,8},{8,12},{12,16},{16,20},{20,24},{24,28},{28,32},{32,36}... | collective-permute-start | bytes 5308424 | tf_op jit(solution)/shard_map/ppermute | solution.py:11
  122.3 47.6 %collective-permute-start.2 = (bf16[768,1152]{1,0:T(8,128)(2,1)}, bf16[768,1152]{1,0:T(8,128)(2,1)}, u32[]{:S(2)}, u32[]{:S(2)}) collective-permute-start(bf16[768,1152]{1,0:T(8,128)(2,1)} %collective-permute-done.1), channel_id=1, source_target_pairs={{0,4},{4,8},{8,12},{12,16},{16,20},{20,24},{24,28},{28,32},{32,36}... | collective-permute-start | bytes 5308424 | tf_op jit(solution)/shard_map/ppermute | solution.py:11
  126.8 2.0 copy-start.5
  126.8 2.0 copy-start.10
  127.1 42.8 %copy-start.2 = (bf16[768,1152]{1,0:T(8,128)(2,1)}, bf16[768,1152]{1,0:T(8,128)(2,1)S(1)}, u32[]{:S(2)}) copy-start(bf16[768,1152]{1,0:T(8,128)(2,1)S(1)} %multiply_convert_fusion.1) | copy-start | bytes 5308420
  132.6 3.6 copy-start.9
  136.1 141.7 %collective-permute-start.3 = (f32[768,1152]{1,0:T(8,128)}, f32[768,1152]{1,0:T(8,128)}, u32[]{:S(2)}, u32[]{:S(2)}) collective-permute-start(f32[768,1152]{1,0:T(8,128)} %fusion.11), channel_id=1, source_target_pairs={{0,4},{4,8},{8,12},{12,16},{16,20},{20,24},{24,28},{28,32},{32,36}... | collective-permute-start | bytes 10616840 | tf_op jit(solution)/shard_map/ppermute | solution.py:11
  138.1 1.8 copy-start.13
  143.3 3.7 copy-start.11
  173.3 3.8 copy-start.6
  189.1 670.2 %all-reduce.2.cloned.1.call-start = ((), (), s32[]{:S(2)}) async-start(), calls=%async_computation.2 | async-start | bytes 3538944 | tf_op jit(solution)/shard_map/psum | solution.py:67
  189.4 97.1 %copy-start.3 = (bf16[768,1152]{1,0:T(8,128)(2,1)S(1)}, bf16[768,1152]{1,0:T(8,128)(2,1)}, u32[]{:S(2)}) copy-start(bf16[768,1152]{1,0:T(8,128)(2,1)} %copy-done.2) | copy-start | bytes 5308420
  189.4 97.1 %copy-start.12 = (bf16[768,768]{1,0:T(8,128)(2,1)S(1)}, bf16[768,768]{1,0:T(8,128)(2,1)}, u32[]{:S(2)}) copy-start(bf16[768,768]{1,0:T(8,128)(2,1)} %copy-done.11) | copy-start | bytes 3538948
  282.6 79.7 %collective-permute-start.4 = (f32[768,1152]{1,0:T(8,128)S(1)}, f32[768,1152]{1,0:T(8,128)S(1)}, u32[]{:S(2)}, u32[]{:S(2)}) collective-permute-start(f32[768,1152]{1,0:T(8,128)S(1)} %convolution_add_fusion), channel_id=1, source_target_pairs={{0,4},{4,8},{8,12},{12,16},{16,20},{20,24},{24,28},{28,32},{32,36}... | collective-permute-start | bytes 10616840 | tf_op jit(solution)/shard_map/ppermute | solution.py:11
  288.3 74.6 %copy-start.7 = (bf16[768,768]{1,0:T(8,128)(2,1)S(1)}, bf16[768,768]{1,0:T(8,128)(2,1)}, u32[]{:S(2)}) copy-start(bf16[768,768]{1,0:T(8,128)(2,1)} %copy-done.6) | copy-start | bytes 3538948
  362.7 78.8 %collective-permute-start.5 = (f32[768,1152]{1,0:T(8,128)S(1)}, f32[768,1152]{1,0:T(8,128)S(1)}, u32[]{:S(2)}, u32[]{:S(2)}) collective-permute-start(f32[768,1152]{1,0:T(8,128)S(1)} %add.83), channel_id=1, source_target_pairs={{0,4},{4,8},{8,12},{12,16},{16,20},{20,24},{24,28},{28,32},{32,36}... | collective-permute-start | bytes 10616840 | tf_op jit(solution)/shard_map/ppermute | solution.py:11
  443.7 421.5 %collective-permute-start.6 = (f32[768,1152]{1,0:T(8,128)}, f32[768,1152]{1,0:T(8,128)}, u32[]{:S(2)}, u32[]{:S(2)}) collective-permute-start(f32[768,1152]{1,0:T(8,128)} %add.84), channel_id=1, source_target_pairs={{0,116},{4,120},{8,124},{12,0},{16,4},{20,8},{24,12},{28,16},{32,2... | collective-permute-start | bytes 10616840 | tf_op jit(solution)/shard_map/ppermute | solution.py:11
Sparse Core Ops, SparseCore 0:
  9.7 58.0 all-gather.1
  189.3 90.3 reduce-scatter.3
  446.9 412.3 all-reduce.1
where the time goes:
time: 880 us; the launch traced here: 879 us
  waiting for transfers between devices  776 us (88%)
  matrix products  43.2 us (5%)
  local copies, waits for them, and re-layouts  17.2 us (2%)
  between operations  15.3 us (2%)
  other arithmetic  15.1 us (2%)
  starting transfers between devices  12.4 us (1%)
    psum x1, waiting for transfers between devices, on_device(): head_grad = lax.psum(head_part, 'dp') / rows  413 us
    ppermute x7, waiting for transfers between devices, passed_along(): lax.ppermute(value, axis, [(i, (i + by) % length) for i in range(length)])  362 us
  transfers between devices with their start and end apart: 10, of which 7 were waited for; matrix products, arithmetic and copies ran while one was open for 7% of the time, Pallas kernels for 0%

commit v1 on v0

v1 whole, which is shorter than its diff:
```python
import jax
import jax.numpy as jnp
from jax import lax
from jax.sharding import Mesh, PartitionSpec as P

AXES = ("x", "y", "zh", "zl", "c")
SIZES = (4, 4, 2, 2, 2)
CONTRACT_ROWS = (((0,), (0,)), ((), ()))
CONTRACT_COLS = (((1,), (1,)), ((), ()))


def index_of(x, y, z, c):
    return ((x % 4 * 4 + y % 4) * 4 + z % 4) * 2 + c


def moved(value, target):
    pairs = [
        (index_of(x, y, z, c), index_of(*target(x, y, z, c)))
        for x in range(4)
        for y in range(4)
        for z in range(4)
        for c in range(2)
    ]
    return lax.ppermute(value, AXES, pairs)


def along_dp(value, by):
    pairs = [(d * 4 + j, (d + by) % 32 * 4 + j) for d in range(32) for j in range(4)]
    return lax.ppermute(value, AXES, pairs)


def unit_rows(vec):
    inv = lax.rsqrt(jnp.sum(vec * vec, axis=-1, keepdims=True) + 1e-06)
    return (vec * inv, inv)


def dot32(a, b, dims=(((1,), (0,)), ((), ()))):
    return lax.dot_general(a, b, dims, preferred_element_type=jnp.float32)


def gathered_head(head):
    x, zl, c = lax.axis_index("x"), lax.axis_index("zl"), lax.axis_index("c")
    half = head.shape[0] // 2
    mine = lax.dynamic_slice_in_dim(head, x % 2 * half, half, 0)
    got = moved(mine, lambda x, y, z, c: (x, y, z ^ 1, c))
    other = moved(got, lambda x, y, z, c: (x ^ 1, y, z, c))
    far = jnp.where(x % 2 == 0, jnp.concatenate([got, other]), jnp.concatenate([other, got]))
    both = jnp.where(zl == 0, jnp.stack([head, far]), jnp.stack([far, head]))
    swapped = moved(both, lambda x, y, z, c: (x, y, z, 1 - c))
    order = jnp.where(c == 0, jnp.stack([both, swapped], 1), jnp.stack([swapped, both], 1))
    return order.reshape(4 * head.shape[0], head.shape[1])


def reduced(part):
    x, zl, c = lax.axis_index("x"), lax.axis_index("zl"), lax.axis_index("c")
    width = part.shape[1]
    f32, b16 = jnp.float32, jnp.bfloat16
    part = part.reshape(2, 2, 288, width)

    def take(value, at, axis):
        return lax.dynamic_index_in_dim(value, at, axis, keepdims=False)

    got = moved(take(part, 1 - c, 1).astype(b16), lambda x, y, z, c: (x, y, z, 1 - c))
    part = take(part, c, 1) + got.astype(f32)
    part = part.reshape(2, 4, 72, width)
    sent = part.astype(b16)
    got = [
        moved(take(sent, (x + d) % 4, 1), lambda x, y, z, c, d=d: (x + d, y, z, c))
        for d in (2, 1, 3)
    ]
    part = take(part, x, 1) + sum(g.astype(f32) for g in got)
    sent = part.astype(b16)
    got = [
        moved(take(sent, (zl + d) % 2, 0), lambda x, y, z, c, d=d: (x, y, z + d, c))
        for d in (2, 1, 3)
    ]
    part = take(part, zl, 0) + sum(g.astype(f32) for g in got)
    sent = part.astype(b16)
    got = [moved(sent, lambda x, y, z, c, d=d: (x, y + d, z, c)) for d in (2, 1, 3)]
    part = part + sum(g.astype(f32) for g in got)
    sent = part.astype(b16)
    got = {d: moved(sent, lambda x, y, z, c, d=d: (x + d, y, z, c)) for d in (2, 1, 3)}
    rel = jnp.stack([sent, got[3], got[2], got[1]])
    rel = jnp.concatenate([rel, rel])
    return lax.dynamic_slice_in_dim(rel, (4 - x) % 4, 4, 0).reshape(288, width).astype(f32)


def on_device(feat, text, head, partner, scale, bias):
    f32, b16 = jnp.float32, jnp.bfloat16
    rows = feat.shape[0]
    feat1 = along_dp(feat, -1)
    text2 = along_dp(text, 2)
    whole = gathered_head(head)
    temper = scale[0]
    offset = bias[0]
    txt_unit, ry = unit_rows(text.astype(f32))
    txt_b = txt_unit.astype(b16)
    txt2_b = unit_rows(text2.astype(f32))[0].astype(b16)
    img0, rx0 = unit_rows(dot32(feat, whole))
    img1, rx1 = unit_rows(dot32(feat1, whole))
    img0_b, img1_b = img0.astype(b16), img1.astype(b16)
    onehot = (partner[:, None] == jnp.arange(rows, dtype=jnp.int32)[None, :]).astype(f32)

    def probability(img_b, txt):
        return jax.nn.sigmoid(temper * dot32(img_b, txt, CONTRACT_COLS) + offset)

    g00 = (probability(img0_b, txt_b) - onehot).astype(b16)
    g02 = probability(img0_b, txt2_b).astype(b16)
    g10 = probability(img1_b, txt_b).astype(b16)
    g12 = probability(img1_b, txt2_b).astype(b16)
    back = dot32(g02, img0_b, CONTRACT_ROWS) + dot32(g12, img1_b, CONTRACT_ROWS)
    back = along_dp(back.astype(b16), -2)

    def projected(img, rx, ga, gb):
        d_img = temper * (dot32(ga, txt_b) + dot32(gb, txt2_b))
        return (rx * (d_img - img * jnp.sum(img * d_img, axis=-1, keepdims=True))).astype(b16)

    part = dot32(feat, projected(img0, rx0, g00, g02), CONTRACT_ROWS)
    part = part + dot32(feat1, projected(img1, rx1, g10, g12), CONTRACT_ROWS)
    head_grad = reduced(part) / rows
    d_txt = dot32(g00, img0_b, CONTRACT_ROWS) + dot32(g10, img1_b, CONTRACT_ROWS)
    d_txt = temper * (d_txt + back.astype(f32))
    text_grad = ry * (d_txt - txt_unit * jnp.sum(txt_unit * d_txt, axis=-1, keepdims=True))
    return (head_grad, text_grad)


def solution(mesh):
    whole = Mesh(mesh.devices.reshape(SIZES), AXES)
    rows = P(AXES, None)
    fsdp = P(("zl", "c"), None)
    return jax.shard_map(
        on_device,
        mesh=whole,
        in_specs=(rows, rows, fsdp, P(AXES), P(), P()),
        out_specs=(fsdp, rows),
        check_vma=False,
    )
```

time: 880 us -> 227 us (0.26)
  the two profiles are of different devices: /device:TPU:0 before, /device:TPU:1 now
where the time goes in v1:
time: 227 us; the launch traced here: 223 us
  waiting for transfers between devices  80.7 us (36%)
  starting transfers between devices  62.8 us (28%)
  matrix products  44.2 us (19%)
  other arithmetic  17.8 us (8%)
  local copies, waits for them, and re-layouts  14.7 us (6%)
  between operations  2.55 us (1%)
    dot_general x16, matrix products, dot32(): return lax.dot_general(a, b, dims, preferred_element_type=jnp.float32)  44.2 us
    ppermute x16, waiting for transfers between devices, moved(): return lax.ppermute(value, AXES, pairs)  42.5 us
    ppermute x3, starting transfers between devices, along_dp(): return lax.ppermute(value, AXES, pairs)  41.2 us
    ppermute x3, waiting for transfers between devices, along_dp(): return lax.ppermute(value, AXES, pairs)  38.2 us
    ppermute x16, starting transfers between devices, moved(): return lax.ppermute(value, AXES, pairs)  21.5 us
    unnamed x46, local copies, waits for them, and re-layouts  11.4 us
  transfers between devices with their start and end apart: 19, of which 13 were waited for; matrix products, arithmetic and copies ran while one was open for 18% of the time, Pallas kernels for 0%

profile of v1, /device:TPU:1, one launch (start us, length us, event | category | flops | bytes accessed | tf_op | source)
XLA Modules:
  0.0 222.8 jit_solution(18343733501151872244)
XLA Ops:
  0.7 1.1 constant_dynamic-slice_fusion
  1.7 2.5 %collective-permute-start = (bf16[144,1152]{1,0:T(8,128)(2,1)S(1)}, bf16[144,1152]{1,0:T(8,128)(2,1)S(1)}, u32[]{:S(2)}, u32[]{:S(2)}) collective-permute-start(bf16[144,1152]{1,0:T(8,128)(2,1)S(1)} %constant_dynamic-slice_fusion), channel_id=1, source_target_pairs={{0,2},{1,3},{2,0},{3,1},{4,6},{5,7},{6,4},{7,5},{8,10},{9,11},{10,... | collective-permute-start | bytes 995336 | tf_op jit(solution)/shard_map/ppermute | solution.py:24
  4.3 1.3 collective-permute-start.3
  5.6 6.2 %collective-permute-done = bf16[144,1152]{1,0:T(8,128)(2,1)S(1)} collective-permute-done((bf16[144,1152]{1,0:T(8,128)(2,1)S(1)}, bf16[144,1152]{1,0:T(8,128)(2,1)S(1)}, u32[]{:S(2)}, u32[]{:S(2)}) %collective-permute-start) | collective-permute-done | bytes 331808 | tf_op jit(solution)/shard_map/ppermute | solution.py:24
  11.8 1.1 collective-permute-start.1
  12.9 6.9 %collective-permute-done.1 = bf16[144,1152]{1,0:T(8,128)(2,1)S(1)} collective-permute-done((bf16[144,1152]{1,0:T(8,128)(2,1)S(1)}, bf16[144,1152]{1,0:T(8,128)(2,1)S(1)}, u32[]{:S(2)}, u32[]{:S(2)}) %collective-permute-start.1) | collective-permute-done | bytes 331808 | tf_op jit(solution)/shard_map/ppermute | solution.py:24
  19.8 1.4 maximum_select_fusion.3
  21.2 1.3 maximum_select_fusion.2
  22.5 2.2 collective-permute-start.2
  24.7 38.2 %collective-permute-start.4 = (bf16[768,1152]{1,0:T(8,128)(2,1)}, bf16[768,1152]{1,0:T(8,128)(2,1)}, u32[]{:S(2)}, u32[]{:S(2)}) collective-permute-start(bf16[768,1152]{1,0:T(8,128)(2,1)} %param.6), channel_id=1, source_target_pairs={{0,124},{1,125},{2,126},{3,127},{4,0},{5,1},{6,2},{7,3},{8,4},{9,5... | collective-permute-start | bytes 5308424 | tf_op jit(solution)/shard_map/ppermute | solution.py:29
  62.9 2.6 %copy.8 = bf16[768,1152]{0,1:T(8,128)(2,1)S(1)} copy(bf16[768,1152]{1,0:T(8,128)(2,1)} %param.7) | data formatting | bytes 3538944 | tf_op args[1]
  66.9 0.4 fusion.8
  67.3 2.3 %maximum_select_fusion.1 = bf16[2,1,288,1152]{3,2,1,0:T(8,128)(2,1)S(1)} fusion(bf16[1,1,288,1152]{3,2,1,0:T(8,128)(2,1)} %bitcast.116, bf16[1,1,288,1152]{3,2,1,0:T(8,128)(2,1)} %bitcast.117, pred[]{:T(512)S(6)} %eq.33), kind=kLoop, calls=%fused_computation.54 | loop fusion | flops 1990656 | bytes 2654209 | tf_op jit(solution)/shard_map/jit(_where)/select_n | solution.py:48
  69.6 0.4 fusion.9
  70.0 2.3 %maximum_select_fusion = bf16[2,2,288,1152]{3,2,1,0:T(8,128)(2,1)S(1)} fusion(bf16[2,1,288,1152]{3,2,1,0:T(8,128)(2,1)} %bitcast.5, bf16[2,1,288,1152]{3,2,1,0:T(8,128)(2,1)S(1)} %maximum_select_fusion.1, pred[]{:T(512)S(6)} %eq.32), kind=kLoop, calls=%fused_computation.38 | loop fusion | flops 3981312 | bytes 5308417 | tf_op jit(solution)/shard_map/jit(_where)/select_n | solution.py:50
  72.4 4.0 %multiply_reduce_fusion.1 = (f32[768]{0:T(1024)S(1)}, f32[1152,768]{1,0:T(8,128)S(1)}) fusion(bf16[1152,1152]{1,0:T(8,128)(2,1)S(1)} %bitcast.119, bf16[768,1152]{1,0:T(8,128)(2,1)} %param.6), kind=kOutput, calls=%fused_computation.36 | convolution fusion | flops 2040200448 | bytes 7965696 | tf_op jit(solution)/shard_map/dot_general | solution.py:38
  76.4 0.3 bitcast_convert_fusion.1
  76.8 0.3 copy-done.16
  77.1 2.2 subtract_convert_fusion
  79.3 1.6 fusion.33
  80.9 20.4 %collective-permute-done.4 = bf16[768,1152]{1,0:T(8,128)(2,1)} collective-permute-done((bf16[768,1152]{1,0:T(8,128)(2,1)}, bf16[768,1152]{1,0:T(8,128)(2,1)}, u32[]{:S(2)}, u32[]{:S(2)}) %collective-permute-start.4) | collective-permute-done | bytes 1769504 | tf_op jit(solution)/shard_map/ppermute | solution.py:29
  101.3 4.0 %multiply_reduce_fusion = (f32[768]{0:T(1024)S(1)}, f32[1152,768]{1,0:T(8,128)S(1)}) fusion(bf16[1152,1152]{1,0:T(8,128)(2,1)S(1)} %bitcast.120, bf16[768,1152]{1,0:T(8,128)(2,1)} %collective-permute-done.4), kind=kOutput, calls=%fused_computation.35 | convolution fusion | flops 2040200448 | bytes 7965696 | tf_op jit(solution)/shard_map/dot_general | solution.py:38
  105.3 0.3 bitcast_convert_fusion
  105.7 2.0 divide_convert_fusion.1
  107.7 1.6 fusion.30
  109.3 2.5 %divide_convert_fusion.2 = bf16[768,768]{1,0:T(8,128)(2,1)S(1)} fusion(bf16[768,1152]{0,1:T(8,128)(2,1)S(1)} %bitcast_convert_fusion.1, f32[]{:T(128)} %bitcast.111, f32[]{:T(128)} %bitcast.107, bf16[768,1152]{1,0:T(8,128)(2,1)S(1)} %collective-permute-done.3, f32[768]{0:T(1024)S(1)} %add_rsqrt_fusion.1), kind=kOutput, calls=%fused_computation.43 | convolution fusion | flops 1365147648 | bytes 4721672 | tf_op jit(solution)/shard_map/dot_general | solution.py:38
  111.9 2.3 %fusion.15 = (f32[768]{0:T(1024)S(1)}, f32[768,1152]{0,1:T(8,128)S(1)}) fusion(f32[1152,768]{1,0:T(8,128)S(1)} %get-tuple-element.15, f32[768]{0:T(1024)S(1)} %add_rsqrt_fusion.3, f32[768,1152]{0,1:T(8,128)S(1)} %fusion.33, bf16[768,768]{1,0:T(8,128)(2,1)S(1)} %divide_convert_fusion.2, bf16[768,1152]{1,0:T(8,128)(2,1)S(1)} %collective-permute-done.3, ...), kind=kOutput, calls=%fused_computation.30 | convolution fusion | flops 1366031616 | bytes 13575172 | tf_op jit(solution)/shard_map/dot_general | solution.py:38
  114.2 4.3 %fusion.20 = f32[1152,1152]{0,1:T(8,128)S(1)} fusion(bf16[768,1152]{1,0:T(8,128)(2,1)} %param.6, f32[768,1152]{0,1:T(8,128)S(1)} %get-tuple-element.17, f32[1152,768]{1,0:T(8,128)S(1)} %get-tuple-element.15, f32[768]{0:T(1024)S(1)} %get-tuple-element.16, f32[768]{0:T(1024)S(1)} %add_rsqrt_fusion.3), kind=kOutput, calls=%fused_computation.46 | convolution fusion | flops 2042855424 | bytes 14161920 | tf_op jit(solution)/shard_map/dot_general | solution.py:38
  118.4 2.1 divide_convert_fusion
  120.6 2.2 fusion.11
  122.8 4.4 %convolution_add_fusion = f32[1152,1152]{0,1:T(8,128)S(1)} fusion(f32[1152,1152]{0,1:T(8,128)S(1)} %fusion.20, bf16[768,1152]{1,0:T(8,128)(2,1)} %collective-permute-done.4, f32[768,1152]{0,1:T(8,128)S(1)} %get-tuple-element.21, f32[1152,768]{1,0:T(8,128)S(1)} %get-tuple-element.19, f32[768]{0:T(1024)S(1)} %get-tuple-element.20, f32[768]{0:T(1024)S(1)} %add_rsqrt_fusion), kind=kOutput, calls=%fused_computation | convolution fusion | flops 2044182528 | bytes 19470336 | tf_op jit(solution)/shard_map/dot_general | solution.py:38
  127.2 2.4 %copy-done = f32[1152,1152]{0,1:T(8,128)} copy-done((f32[1152,1152]{0,1:T(8,128)}, f32[1152,1152]{0,1:T(8,128)S(1)}, u32[]{:S(2)}) %copy-start) | copy-done | bytes 5308440
  129.6 1.2 fusion.29
  130.8 0.8 collective-permute-start.5
  131.6 3.0 %fusion.43 = f32[768,1152]{0,1:T(8,128)S(1)} fusion(bf16[768,1152]{0,1:T(8,128)(2,1)S(1)} %copy-done.8, bf16[768,768]{1,0:T(8,128)(2,1)} %copy-done.14), kind=kOutput, calls=%fused_computation.85 | convolution fusion | flops 1358954496 | bytes 6488064 | tf_op jit(solution)/shard_map/dot_general | solution.py:38
  134.7 1.7 bitcast_add_fusion
  136.5 1.0 dynamic-slice_bitcast_fusion.2
  137.5 0.7 copy-done.2
  138.2 1.5 collective-permute-start.7
  139.7 0.5 collective-permute-start.6
  140.2 2.9 %fusion.19 = bf16[768,1152]{0,1:T(8,128)(2,1)} fusion(f32[768,1152]{0,1:T(8,128)S(1)} %fusion.43, bf16[768,1152]{0,1:T(8,128)(2,1)S(1)} %copy-done.4, bf16[768,768]{1,0:T(8,128)(2,1)S(1)} %copy-done.13), kind=kOutput, calls=%fused_computation.37 | convolution fusion | flops 1360723968 | bytes 8257536 | tf_op jit(solution)/shard_map/dot_general | solution.py:38
  143.1 1.7 collective-permute-start.18
  144.8 2.7 %collective-permute-done.8 = bf16[2,72,1152]{2,1,0:T(8,128)(2,1)} collective-permute-done((bf16[2,72,1152]{2,1,0:T(8,128)(2,1)}, bf16[2,72,1152]{2,1,0:T(8,128)(2,1)}, u32[]{:S(2)}, u32[]{:S(2)}) %collective-permute-start.8) | collective-permute-done | bytes 331808 | tf_op jit(solution)/shard_map/ppermute | solution.py:24
  147.5 2.2 %collective-permute-done.7 = bf16[2,72,1152]{2,1,0:T(8,128)(2,1)} collective-permute-done((bf16[2,72,1152]{2,1,0:T(8,128)(2,1)}, bf16[2,72,1152]{2,1,0:T(8,128)(2,1)}, u32[]{:S(2)}, u32[]{:S(2)}) %collective-permute-start.7) | collective-permute-done | bytes 331808 | tf_op jit(solution)/shard_map/ppermute | solution.py:24
  149.7 5.1 %collective-permute-done.6 = bf16[2,72,1152]{2,1,0:T(8,128)(2,1)} collective-permute-done((bf16[2,72,1152]{2,1,0:T(8,128)(2,1)}, bf16[2,72,1152]{2,1,0:T(8,128)(2,1)}, u32[]{:S(2)}, u32[]{:S(2)}) %collective-permute-start.6) | collective-permute-done | bytes 331808 | tf_op jit(solution)/shard_map/ppermute | solution.py:24
  154.9 1.5 fusion.41
  156.5 1.5 collective-permute-start.10
  158.0 1.6 fusion.42
  159.6 1.5 collective-permute-done.11
  161.1 0.9 collective-permute-done.10
  162.0 3.0 %collective-permute-done.9 = bf16[72,1152]{1,0:T(8,128)(2,1)S(1)} collective-permute-done((bf16[72,1152]{1,0:T(8,128)(2,1)S(1)}, bf16[72,1152]{1,0:T(8,128)(2,1)S(1)}, u32[]{:S(2)}, u32[]{:S(2)}) %collective-permute-start.9) | collective-permute-done | bytes 165920 | tf_op jit(solution)/shard_map/ppermute | solution.py:24
  165.1 8.3 %collective-permute-start.14 = (bf16[72,1152]{1,0:T(8,128)(2,1)S(1)}, bf16[72,1152]{1,0:T(8,128)(2,1)S(1)}, u32[]{:S(2)}, u32[]{:S(2)}) collective-permute-start(bf16[72,1152]{1,0:T(8,128)(2,1)S(1)} %fusion.36), channel_id=1, source_target_pairs={{0,24},{1,25},{2,26},{3,27},{4,28},{5,29},{6,30},{7,31},{8,0},{9,1... | collective-permute-start | bytes 497672 | tf_op jit(solution)/shard_map/ppermute | solution.py:24
  173.4 1.3 collective-permute-start.12
  174.7 17.8 %collective-permute-done.18 = bf16[768,1152]{0,1:T(8,128)(2,1)} collective-permute-done((bf16[768,1152]{0,1:T(8,128)(2,1)}, bf16[768,1152]{0,1:T(8,128)(2,1)}, u32[]{:S(2)}, u32[]{:S(2)}) %collective-permute-start.18) | collective-permute-done | bytes 1769504 | tf_op jit(solution)/shard_map/ppermute | solution.py:29
  192.5 3.5 %fusion.5 = (f32[768]{0:T(1024)S(1)}, f32[768,1152]{0,1:T(8,128)S(1)}) fusion(bf16[768,1152]{0,1:T(8,128)(2,1)S(1)} %copy.8, bf16[768,1152]{0,1:T(8,128)(2,1)} %collective-permute-done.18, f32[768]{0:T(1024)S(1)} %add_rsqrt_fusion.2, f32[]{:T(128)} %bitcast.103, f32[768,1152]{0,1:T(8,128)S(1)} %fusion.42, bf16[768,1152]{0,1:T(8,128)(2,1)S(1)} %copy-done.4, ...), kind=kOutput, calls=%fused_computation.14 | convolution fusion | flops 1366031616 | bytes 13572100 | tf_op jit(solution)/shard_map/dot_general | solution.py:38
  196.1 3.2 %collective-permute-done.14 = bf16[72,1152]{1,0:T(8,128)(2,1)S(1)} collective-permute-done((bf16[72,1152]{1,0:T(8,128)(2,1)S(1)}, bf16[72,1152]{1,0:T(8,128)(2,1)S(1)}, u32[]{:S(2)}, u32[]{:S(2)}) %collective-permute-start.14) | collective-permute-done | bytes 165920 | tf_op jit(solution)/shard_map/ppermute | solution.py:24
  199.4 1.2 collective-permute-start.15
  200.7 4.2 %fusion.7 = f32[768,1152]{0,1:T(8,128)} fusion(bf16[768,1152]{0,1:T(8,128)(2,1)S(1)} %copy.8, f32[768,1152]{0,1:T(8,128)S(1)} %get-tuple-element.23, bf16[768,1152]{0,1:T(8,128)(2,1)} %collective-permute-done.18, f32[768]{0:T(1024)S(1)} %get-tuple-element.22, f32[768]{0:T(1024)S(1)} %add_rsqrt_fusion.2, f32[]{:T(128)} %bitcast.102), kind=kLoop, calls=%fused_computation.16 | loop fusion | flops 7077888 | bytes 10622980 | tf_op jit(solution)/shard_map/mul | solution.py:123
  204.9 5.2 %copy.17 = f32[768,1152]{1,0:T(8,128)} copy(f32[768,1152]{0,1:T(8,128)} %fusion.7) | data formatting | bytes 7077888
  210.1 0.4 collective-permute-start.16
  210.4 0.2 collective-permute-start.17
  210.7 5.9 %collective-permute-done.16 = bf16[72,1152]{1,0:T(8,128)(2,1)S(1)} collective-permute-done((bf16[72,1152]{1,0:T(8,128)(2,1)S(1)}, bf16[72,1152]{1,0:T(8,128)(2,1)S(1)}, u32[]{:S(2)}, u32[]{:S(2)}) %collective-permute-start.16) | collective-permute-done | bytes 165920 | tf_op jit(solution)/shard_map/ppermute | solution.py:24
  216.6 4.7 %collective-permute-done.17 = bf16[72,1152]{1,0:T(8,128)(2,1)S(1)} collective-permute-done((bf16[72,1152]{1,0:T(8,128)(2,1)S(1)}, bf16[72,1152]{1,0:T(8,128)(2,1)S(1)}, u32[]{:S(2)}, u32[]{:S(2)}) %collective-permute-start.17) | collective-permute-done | bytes 165920 | tf_op jit(solution)/shard_map/ppermute | solution.py:24
  221.4 1.2 convert_multiply_fusion.4
  (60 shorter events, 0.8 us)
Async XLA Ops:
  0.6 20.6 %copy-start.6 = (bf16[288,1152]{1,0:T(8,128)(2,1)S(1)}, bf16[288,1152]{1,0:T(8,128)(2,1)}, u32[]{:S(2)}) copy-start(bf16[288,1152]{1,0:T(8,128)(2,1)} %param.8) | copy-start | bytes 1990660
  1.7 10.0 %collective-permute-start = (bf16[144,1152]{1,0:T(8,128)(2,1)S(1)}, bf16[144,1152]{1,0:T(8,128)(2,1)S(1)}, u32[]{:S(2)}, u32[]{:S(2)}) collective-permute-start(bf16[144,1152]{1,0:T(8,128)(2,1)S(1)} %constant_dynamic-slice_fusion), channel_id=1, source_target_pairs={{0,2},{1,3},{2,0},{3,1},{4,6},{5,7},{6,4},{7,5},{8,10},{9,11},{10,... | collective-permute-start | bytes 995336 | tf_op jit(solution)/shard_map/ppermute | solution.py:24
  4.3 65.3 %collective-permute-start.3 = (bf16[768,1152]{1,0:T(8,128)(2,1)}, bf16[768,1152]{1,0:T(8,128)(2,1)S(1)}, u32[]{:S(2)}, u32[]{:S(2)}) collective-permute-start(bf16[768,1152]{1,0:T(8,128)(2,1)} %param.7), channel_id=1, source_target_pairs={{0,8},{1,9},{2,10},{3,11},{4,12},{5,13},{6,14},{7,15},{8,16},{9,17... | collective-permute-start | bytes 5308424 | tf_op jit(solution)/shard_map/ppermute | solution.py:29
  11.8 8.0 %copy-start.15 = (bf16[144,1152]{1,0:T(8,128)(2,1)}, bf16[144,1152]{1,0:T(8,128)(2,1)S(1)}, u32[]{:S(2)}) copy-start(bf16[144,1152]{1,0:T(8,128)(2,1)S(1)} %collective-permute-done) | copy-start | bytes 995332
  11.8 8.0 %collective-permute-start.1 = (bf16[144,1152]{1,0:T(8,128)(2,1)S(1)}, bf16[144,1152]{1,0:T(8,128)(2,1)S(1)}, u32[]{:S(2)}, u32[]{:S(2)}) collective-permute-start(bf16[144,1152]{1,0:T(8,128)(2,1)S(1)} %collective-permute-done), channel_id=1, source_target_pairs={{0,32},{1,33},{2,34},{3,35},{4,36},{5,37},{6,38},{7,39},{8,40},{9,... | collective-permute-start | bytes 995336 | tf_op jit(solution)/shard_map/ppermute | solution.py:24
  21.2 41.8 %copy-start.5 = (bf16[1,288,1152]{2,1,0:T(8,128)(2,1)}, bf16[1,288,1152]{2,1,0:T(8,128)(2,1)S(1)}, u32[]{:S(2)}) copy-start(bf16[1,288,1152]{2,1,0:T(8,128)(2,1)S(1)} %maximum_select_fusion.3) | copy-start | bytes 1990660
  22.5 47.5 %collective-permute-start.2 = (bf16[2,288,1152]{2,1,0:T(8,128)(2,1)}, bf16[2,288,1152]{2,1,0:T(8,128)(2,1)}, u32[]{:S(2)}, u32[]{:S(2)}) collective-permute-start(bf16[2,288,1152]{2,1,0:T(8,128)(2,1)} %maximum_select_fusion.2), channel_id=1, source_target_pairs={{0,1},{1,0},{2,3},{3,2},{4,5},{5,4},{6,7},{7,6},{8,9},{9,8},{10,11... | collective-permute-start | bytes 3981320 | tf_op jit(solution)/shard_map/ppermute | solution.py:24
  24.7 76.6 %collective-permute-start.4 = (bf16[768,1152]{1,0:T(8,128)(2,1)}, bf16[768,1152]{1,0:T(8,128)(2,1)}, u32[]{:S(2)}, u32[]{:S(2)}) collective-permute-start(bf16[768,1152]{1,0:T(8,128)(2,1)} %param.6), channel_id=1, source_target_pairs={{0,124},{1,125},{2,126},{3,127},{4,0},{5,1},{6,2},{7,3},{8,4},{9,5... | collective-permute-start | bytes 5308424 | tf_op jit(solution)/shard_map/ppermute | solution.py:29
  76.4 0.7 copy-start.16
  76.7 32.6 %copy-start.7 = (bf16[768,1152]{0,1:T(8,128)(2,1)}, bf16[768,1152]{0,1:T(8,128)(2,1)S(1)}, u32[]{:S(2)}) copy-start(bf16[768,1152]{0,1:T(8,128)(2,1)S(1)} %bitcast_convert_fusion.1) | copy-start | bytes 5308420
  79.3 1.6 copy-start.17
  105.7 12.8 %copy-start.3 = (bf16[768,1152]{0,1:T(8,128)(2,1)}, bf16[768,1152]{0,1:T(8,128)(2,1)S(1)}, u32[]{:S(2)}) copy-start(bf16[768,1152]{0,1:T(8,128)(2,1)S(1)} %bitcast_convert_fusion) | copy-start | bytes 5308420
  107.7 1.6 copy-start.10
  111.9 2.3 %copy-start.14 = (bf16[768,768]{1,0:T(8,128)(2,1)}, bf16[768,768]{1,0:T(8,128)(2,1)S(1)}, u32[]{:S(2)}) copy-start(bf16[768,768]{1,0:T(8,128)(2,1)S(1)} %divide_convert_fusion.2) | copy-start | bytes 3538948
  120.6 2.2 copy-start.12
  127.2 2.4 %copy-start = (f32[1152,1152]{0,1:T(8,128)}, f32[1152,1152]{0,1:T(8,128)S(1)}, u32[]{:S(2)}) copy-start(f32[1152,1152]{0,1:T(8,128)S(1)} %convolution_add_fusion) | copy-start | bytes 15925252
  127.2 4.4 %copy-start.8 = (bf16[768,1152]{0,1:T(8,128)(2,1)S(1)}, bf16[768,1152]{0,1:T(8,128)(2,1)}, u32[]{:S(2)}) copy-start(bf16[768,1152]{0,1:T(8,128)(2,1)} %copy-done.7) | copy-start | bytes 5308420
  130.8 3.8 %collective-permute-start.5 = (bf16[2,288,1152]{2,1,0:T(8,128)(2,1)}, bf16[2,288,1152]{2,1,0:T(8,128)(2,1)}, u32[]{:S(2)}, u32[]{:S(2)}) collective-permute-start(bf16[2,288,1152]{2,1,0:T(8,128)(2,1)} %fusion.29), channel_id=1, source_target_pairs={{0,1},{1,0},{2,3},{3,2},{4,5},{5,4},{6,7},{7,6},{8,9},{9,8},{10,11... | collective-permute-start | bytes 3981320 | tf_op jit(solution)/shard_map/ppermute | solution.py:24
  131.6 3.0 %copy-start.1 = (f32[1152,1152]{0,1:T(8,128)S(1)}, f32[1152,1152]{0,1:T(8,128)}, u32[]{:S(2)}) copy-start(f32[1152,1152]{0,1:T(8,128)} %copy-done) | copy-start | bytes 15925252
  136.3 1.9 copy-start.2
  136.3 3.8 %copy-start.4 = (bf16[768,1152]{0,1:T(8,128)(2,1)S(1)}, bf16[768,1152]{0,1:T(8,128)(2,1)}, u32[]{:S(2)}) copy-start(bf16[768,1152]{0,1:T(8,128)(2,1)} %copy-done.3) | copy-start | bytes 5308420
  136.3 3.8 %copy-start.13 = (bf16[768,768]{1,0:T(8,128)(2,1)S(1)}, bf16[768,768]{1,0:T(8,128)(2,1)}, u32[]{:S(2)}) copy-start(bf16[768,768]{1,0:T(8,128)(2,1)} %copy-done.12) | copy-start | bytes 3538948
  138.2 9.3 %collective-permute-start.8 = (bf16[2,72,1152]{2,1,0:T(8,128)(2,1)}, bf16[2,72,1152]{2,1,0:T(8,128)(2,1)}, u32[]{:S(2)}, u32[]{:S(2)}) collective-permute-start(bf16[2,72,1152]{2,1,0:T(8,128)(2,1)} %get-tuple-element.9), channel_id=1, source_target_pairs={{0,96},{1,97},{2,98},{3,99},{4,100},{5,101},{6,102},{7,103},{8,104... | collective-permute-start | bytes 995336 | tf_op jit(solution)/shard_map/ppermute | solution.py:24
  138.2 11.6 %collective-permute-start.7 = (bf16[2,72,1152]{2,1,0:T(8,128)(2,1)}, bf16[2,72,1152]{2,1,0:T(8,128)(2,1)}, u32[]{:S(2)}, u32[]{:S(2)}) collective-permute-start(bf16[2,72,1152]{2,1,0:T(8,128)(2,1)} %get-tuple-element.10), channel_id=1, source_target_pairs={{0,32},{1,33},{2,34},{3,35},{4,36},{5,37},{6,38},{7,39},{8,40},{9,... | collective-permute-start | bytes 995336 | tf_op jit(solution)/shard_map/ppermute | solution.py:24
  139.7 15.2 %collective-permute-start.6 = (bf16[2,72,1152]{2,1,0:T(8,128)(2,1)}, bf16[2,72,1152]{2,1,0:T(8,128)(2,1)}, u32[]{:S(2)}, u32[]{:S(2)}) collective-permute-start(bf16[2,72,1152]{2,1,0:T(8,128)(2,1)} %get-tuple-element.8), channel_id=1, source_target_pairs={{0,64},{1,65},{2,66},{3,67},{4,68},{5,69},{6,70},{7,71},{8,72},{9,... | collective-permute-start | bytes 995336 | tf_op jit(solution)/shard_map/ppermute | solution.py:24
  143.1 49.5 %collective-permute-start.18 = (bf16[768,1152]{0,1:T(8,128)(2,1)}, bf16[768,1152]{0,1:T(8,128)(2,1)}, u32[]{:S(2)}, u32[]{:S(2)}) collective-permute-start(bf16[768,1152]{0,1:T(8,128)(2,1)} %fusion.19), channel_id=1, source_target_pairs={{0,120},{1,121},{2,122},{3,123},{4,124},{5,125},{6,126},{7,127},{8... | collective-permute-start | bytes 5308424 | tf_op jit(solution)/shard_map/ppermute | solution.py:29
  144.8 13.2 %copy-start.9 = (bf16[768,1152]{0,1:T(8,128)(2,1)S(1)}, bf16[768,1152]{0,1:T(8,128)(2,1)}, u32[]{:S(2)}) copy-start(bf16[768,1152]{0,1:T(8,128)(2,1)} %copy-done.7) | copy-start | bytes 5308420
  144.8 13.2 %copy-start.18 = (bf16[768,768]{1,0:T(8,128)(2,1)S(1)}, bf16[768,768]{1,0:T(8,128)(2,1)}, u32[]{:S(2)}) copy-start(bf16[768,768]{1,0:T(8,128)(2,1)} %copy-done.17) | copy-start | bytes 3538948
  156.5 4.7 %collective-permute-start.11 = (bf16[72,1152]{1,0:T(8,128)(2,1)S(1)}, bf16[72,1152]{1,0:T(8,128)(2,1)S(1)}, u32[]{:S(2)}, u32[]{:S(2)}) collective-permute-start(bf16[72,1152]{1,0:T(8,128)(2,1)S(1)} %get-tuple-element.12), channel_id=1, source_target_pairs={{0,6},{1,7},{2,0},{3,1},{4,2},{5,3},{6,4},{7,5},{8,14},{9,15},{10,... | collective-permute-start | bytes 497672 | tf_op jit(solution)/shard_map/ppermute | solution.py:24
  156.5 5.5 %collective-permute-start.10 = (bf16[72,1152]{1,0:T(8,128)(2,1)S(1)}, bf16[72,1152]{1,0:T(8,128)(2,1)S(1)}, u32[]{:S(2)}, u32[]{:S(2)}) collective-permute-start(bf16[72,1152]{1,0:T(8,128)(2,1)S(1)} %get-tuple-element.13), channel_id=1, source_target_pairs={{0,2},{1,3},{2,4},{3,5},{4,6},{5,7},{6,0},{7,1},{8,10},{9,11},{10,... | collective-permute-start | bytes 497672 | tf_op jit(solution)/shard_map/ppermute | solution.py:24
  158.0 34.5 %copy-start.11 = (bf16[768,768]{1,0:T(8,128)(2,1)S(1)}, bf16[768,768]{1,0:T(8,128)(2,1)}, u32[]{:S(2)}) copy-start(bf16[768,768]{1,0:T(8,128)(2,1)} %copy-done.10) | copy-start | bytes 3538948
  158.0 7.0 %collective-permute-start.9 = (bf16[72,1152]{1,0:T(8,128)(2,1)S(1)}, bf16[72,1152]{1,0:T(8,128)(2,1)S(1)}, u32[]{:S(2)}, u32[]{:S(2)}) collective-permute-start(bf16[72,1152]{1,0:T(8,128)(2,1)S(1)} %get-tuple-element.11), channel_id=1, source_target_pairs={{0,4},{1,5},{2,6},{3,7},{4,0},{5,1},{6,2},{7,3},{8,12},{9,13},{10,... | collective-permute-start | bytes 497672 | tf_op jit(solution)/shard_map/ppermute | solution.py:24
  165.1 34.2 %collective-permute-start.14 = (bf16[72,1152]{1,0:T(8,128)(2,1)S(1)}, bf16[72,1152]{1,0:T(8,128)(2,1)S(1)}, u32[]{:S(2)}, u32[]{:S(2)}) collective-permute-start(bf16[72,1152]{1,0:T(8,128)(2,1)S(1)} %fusion.36), channel_id=1, source_target_pairs={{0,24},{1,25},{2,26},{3,27},{4,28},{5,29},{6,30},{7,31},{8,0},{9,1... | collective-permute-start | bytes 497672 | tf_op jit(solution)/shard_map/ppermute | solution.py:24
  173.4 25.9 %collective-permute-start.13 = (bf16[72,1152]{1,0:T(8,128)(2,1)S(1)}, bf16[72,1152]{1,0:T(8,128)(2,1)S(1)}, u32[]{:S(2)}, u32[]{:S(2)}) collective-permute-start(bf16[72,1152]{1,0:T(8,128)(2,1)S(1)} %fusion.36), channel_id=1, source_target_pairs={{0,8},{1,9},{2,10},{3,11},{4,12},{5,13},{6,14},{7,15},{8,16},{9,17... | collective-permute-start | bytes 497672 | tf_op jit(solution)/shard_map/ppermute | solution.py:24
  173.4 25.9 %collective-permute-start.12 = (bf16[72,1152]{1,0:T(8,128)(2,1)S(1)}, bf16[72,1152]{1,0:T(8,128)(2,1)S(1)}, u32[]{:S(2)}, u32[]{:S(2)}) collective-permute-start(bf16[72,1152]{1,0:T(8,128)(2,1)S(1)} %fusion.36), channel_id=1, source_target_pairs={{0,16},{1,17},{2,18},{3,19},{4,20},{5,21},{6,22},{7,23},{8,24},{9,... | collective-permute-start | bytes 497672 | tf_op jit(solution)/shard_map/ppermute | solution.py:24
  199.4 11.2 %collective-permute-start.15 = (bf16[72,1152]{1,0:T(8,128)(2,1)S(1)}, bf16[72,1152]{1,0:T(8,128)(2,1)S(1)}, u32[]{:S(2)}, u32[]{:S(2)}) collective-permute-start(bf16[72,1152]{1,0:T(8,128)(2,1)S(1)} %get-tuple-element.5), channel_id=1, source_target_pairs={{0,96},{1,97},{2,98},{3,99},{4,100},{5,101},{6,102},{7,103},{8,104... | collective-permute-start | bytes 497672 | tf_op jit(solution)/shard_map/ppermute | solution.py:24
  210.1 6.5 %collective-permute-start.16 = (bf16[72,1152]{1,0:T(8,128)(2,1)S(1)}, bf16[72,1152]{1,0:T(8,128)(2,1)S(1)}, u32[]{:S(2)}, u32[]{:S(2)}) collective-permute-start(bf16[72,1152]{1,0:T(8,128)(2,1)S(1)} %get-tuple-element.5), channel_id=1, source_target_pairs={{0,64},{1,65},{2,66},{3,67},{4,68},{5,69},{6,70},{7,71},{8,72},{9,... | collective-permute-start | bytes 497672 | tf_op jit(solution)/shard_map/ppermute | solution.py:24
  210.4 10.9 %collective-permute-start.17 = (bf16[72,1152]{1,0:T(8,128)(2,1)S(1)}, bf16[72,1152]{1,0:T(8,128)(2,1)S(1)}, u32[]{:S(2)}, u32[]{:S(2)}) collective-permute-start(bf16[72,1152]{1,0:T(8,128)(2,1)S(1)} %get-tuple-element.5), channel_id=1, source_target_pairs={{0,32},{1,33},{2,34},{3,35},{4,36},{5,37},{6,38},{7,39},{8,40},{9,... | collective-permute-start | bytes 497672 | tf_op jit(solution)/shard_map/ppermute | solution.py:24
